TPU v7x, 512 devices: a whole 4x8x8 slice. The times are simulated.
512 devices in a mesh: row: 64 (over x, z, core), col: 8 (over y).
Axes of the slice: x: 4, y: 8, z: 8, core: 2. Of those that a mesh axis runs over, the one named last changes fastest.
Arguments:
- features: bfloat16 [262144, 512], P(('row', 'col')), may hold values from -6 to 6
- factor: float32 [262144, 1024], P(('row', 'col')), may hold values from -0.03 to 0.03
- ip_weights: float32 [262144], P(('row', 'col')), may hold values from 0.1 to 30
- pivot_owner: int32 [256], replicated, may hold values from 0 to 511, as said below
- pivot_position: int32 [256], replicated, may hold values from 0 to 511, as said below
Outputs:
- new_columns: float32 [262144, 256], P(('row', 'col'))
- gram_rows: float32 [256, 1280], replicated
Inputs may be any that keep to these rules, and one draw needn't show every extreme that they name: `pivot_owner`: each device owns at most 3 pivots, and some device owns exactly 3. `pivot_position`: pivots with the same owner have different positions.
All inputs are finite; a program needn't handle non-finite values.
Results may differ from a plain program's by a relative error of at most 0.0003.
Values may be sent and summed in bfloat16 or wider, within the bound.
A program may use at most 64 MiB of HBM per device.

v0:
```python
import jax
import jax.numpy as jnp
from jax import lax
from jax.sharding import Mesh
from jax.sharding import PartitionSpec as P

F = 512
ROW = ("row_0", "row_1", "row_2")
ROW_COL = ("row_0", "row_1", "row_2", "col")
kernel_rates = (0.25, 0.5, 1.0)
kernel_mixes = (0.5, 0.3, 0.2)


def copy_for_each(array, axis):
    copies = jnp.broadcast_to(array, (lax.axis_size(axis), *array.shape))
    return lax.all_to_all(copies, axis, split_axis=0, concat_axis=0, tiled=True)


def in_order(parts, dim):
    dims = list(parts.shape[1:])
    dims[dim] *= parts.shape[0]
    return jnp.moveaxis(parts, 0, dim).reshape(dims)


def gather_axes(array, axes, dim):
    far, near = axes
    parts = copy_for_each(copy_for_each(array, far), near)
    return in_order(parts.swapaxes(0, 1).reshape(-1, *array.shape), dim)


def cut_along(array, dim, length):
    before, after = (array.shape[:dim], array.shape[dim + 1 :])
    return jnp.moveaxis(array.reshape(*before, length, -1, *after), dim, 0)


def summed_on_arrival(array, axis, dim):
    parts = cut_along(array, dim, lax.axis_size(axis))
    arrived = lax.all_to_all(parts, axis, split_axis=0, concat_axis=0, tiled=True)
    return arrived.sum(axis=0)


def sum_by_axis(array, axes, dim):
    far, near = axes
    own = summed_on_arrival(cut_along(array, dim, lax.axis_size(far)), near, dim + 1)
    return jnp.sum(lax.all_to_all(own, far, 0, 0, tiled=True), axis=0)


def rows_for(lines, length):
    spare = -lines.shape[0] % length
    if not spare:
        return lines
    return jnp.concatenate([lines, jnp.zeros((spare, *lines.shape[1:]), lines.dtype)])


def total_of(array, axes):
    lines = array.reshape(-1)
    own = sum_by_axis(rows_for(lines, lax.axis_size(axes[0]) * lax.axis_size(axes[1])), axes, 0)
    whole = gather_axes(own, axes, 0)
    return whole[: len(lines)].reshape(array.shape)


def kernel_of(left, right):
    cross_term = jnp.dot(left, right.T, preferred_element_type=jnp.float32)
    left_norms = jnp.sum(jnp.square(left.astype(jnp.float32)), axis=1)
    right_norms = jnp.sum(jnp.square(right.astype(jnp.float32)), axis=1)
    distance = left_norms[:, None] + right_norms[None, :] - 2.0 * cross_term
    total = jnp.zeros_like(distance)
    for rate, mixing in zip(kernel_rates, kernel_mixes):
        total = total + mixing * jnp.exp(-(rate / F) * distance)
    return total


def body(features, factor, ip_weights, pivot_owner, pivot_position):
    devices = lax.axis_size(ROW) * lax.axis_size("col")
    device_rank = lax.axis_index(ROW) * lax.axis_size("col") + lax.axis_index("col")
    pivot_count = pivot_owner.shape[0]
    slot_count = 2 * pivot_count // devices + 2
    same_owner = pivot_owner[:, None] == pivot_owner[None, :]
    earlier = jnp.arange(pivot_count)[None, :] < jnp.arange(pivot_count)[:, None]
    slot_rank = jnp.sum((same_owner & earlier).astype(jnp.int32), axis=1)
    chosen = (pivot_owner == device_rank)[None, :] & (
        slot_rank[None, :] == jnp.arange(slot_count)[:, None]
    )
    filled = jnp.any(chosen, axis=1)[:, None]
    slot_rows = jnp.sum(jnp.where(chosen, pivot_position[None, :], 0), axis=1)
    slot_x = jnp.where(filled, features[slot_rows], jnp.zeros((), jnp.bfloat16))
    slot_h = jnp.where(filled, factor[slot_rows], 0.0)
    every_x = gather_axes(slot_x, (("row_0", "row_1"), ("row_2", "col")), 0)
    every_h = lax.all_gather(slot_h, ROW_COL, axis=0, tiled=True)
    source = pivot_owner * slot_count + slot_rank
    pivot_x = every_x[source]
    pivot_h = every_h[source]
    residual = kernel_of(features, pivot_x) - jnp.dot(
        factor, pivot_h.T, precision=lax.Precision.HIGHEST
    )
    block = kernel_of(pivot_x, pivot_x) - jnp.dot(
        pivot_h, pivot_h.T, precision=lax.Precision.HIGHEST
    )
    lower_block = jnp.linalg.cholesky(block)
    new_columns = jax.scipy.linalg.solve_triangular(lower_block, residual.T, lower=True).T
    weighted = new_columns * ip_weights[:, None]
    left_part = jnp.dot(weighted.T, factor, precision=lax.Precision.HIGHEST)
    right_part = jnp.dot(weighted.T, new_columns, precision=lax.Precision.HIGHEST)
    local_gram = jnp.concatenate([left_part, right_part], axis=1)
    summed = total_of(local_gram, (("row_0", "row_1"), ("row_2", "col")))
    total_samples = features.shape[0] * devices
    return (new_columns, summed / total_samples)


def solution(mesh):
    torus = Mesh(
        mesh.devices.reshape(4, 8, 2, mesh.shape["col"]), ("row_0", "row_1", "row_2", "col")
    )
    in_specs = (P(ROW_COL, None), P(ROW_COL, None), P(ROW_COL), P(), P())
    out_specs = (P(ROW_COL, None), P())
    return jax.shard_map(body, mesh=torus, in_specs=in_specs, out_specs=out_specs, check_vma=False)
```

profile of v0, /device:TPU:1, one launch (start us, length us, event | category | flops | bytes accessed | tf_op | source)
XLA Modules:
  0.0 362.9 jit_solution(6088916679859474437)
XLA Ops:
  7.2 1.0 convert_reduce_fusion
  8.2 0.7 broadcast_compare_fusion
  9.1 0.8 select_reduce_fusion.2
  9.9 0.6 gather_fusion.2
  10.4 0.7 select_bitcast_fusion.1
  11.2 1.7 gather_fusion
  13.0 22.7 %all_to_all.38 = bf16[32,3,512]{2,1,0:T(4,128)(2,1)S(1)} all-to-all(bf16[32,3,512]{2,1,0:T(4,128)(2,1)S(1)} %broadcast_in_dim.74), channel_id=1, replica_groups=mesh['row_0'=4,'row_1'=8,'row_2'=2,'col'=8] {'row_0','row_1'}, dimensions={0} | all-to-all | bytes 196608 | tf_op jit(solution)/shard_map/all_to_all | solution.py:16
  35.6 1.4 broadcast_in_dim.75
  37.1 9.3 %all-to-all-start.1 = ((bf16[16,32,3,512]{3,1,2,0:T(8,128)(2,1)}), bf16[16,32,3,512]{3,1,2,0:T(8,128)(2,1)}, u32[]{:S(2)}, u32[]{:S(2)}) async-start(bf16[16,32,3,512]{3,1,2,0:T(8,128)(2,1)} %broadcast_in_dim.75), calls=%async_computation.1 | async-start | bytes 3145728 | tf_op jit(solution)/shard_map/all_to_all | solution.py:16
  46.6 37.9 %all-to-all-done.1 = bf16[16,32,3,512]{3,1,2,0:T(8,128)(2,1)} async-done(((bf16[16,32,3,512]{3,1,2,0:T(8,128)(2,1)}), bf16[16,32,3,512]{3,1,2,0:T(8,128)(2,1)}, u32[]{:S(2)}, u32[]{:S(2)}) %all-to-all-start.1) | async-done | bytes 1572896 | tf_op jit(solution)/shard_map/all_to_all | solution.py:16
  84.5 4.2 %copy.42 = bf16[32,16,3,512]{3,2,1,0:T(4,128)(2,1)} copy(bf16[32,16,3,512]{3,0,2,1:T(8,128)(2,1)} %bitcast.2) | data formatting | bytes 3145728 | tf_op jit(solution)/shard_map/transpose | solution.py:28
  88.6 5.1 %reshape_reshape.3 = bf16[1536,512]{1,0:T(8,128)(2,1)} reshape(bf16[32,16,3,512]{3,2,1,0:T(4,128)(2,1)} %copy.42) | data formatting | bytes 3145728 | tf_op jit(solution)/shard_map/reshape;reshape | solution.py:22
  93.7 2.8 gather_fusion.1
  96.8 0.8 copy.44
  97.8 1.1 fusion
  98.9 55.2 %all-gather.3.cloned.1.call-done = f32[512,3,1024]{2,1,0:T(4,128)} async-done(((f32[1,3,1024]{2,1,0:T(4,128)}), f32[512,3,1024]{2,1,0:T(4,128)}) %all-gather.3.cloned.1.call-update) | async-done | bytes 6291472 | tf_op jit(solution)/shard_map/all_gather | solution.py:89
  154.1 10.8 %reshape.108 = f32[1536,1024]{1,0:T(8,128)} reshape(f32[512,3,1024]{2,1,0:T(4,128)} %all-gather.3.cloned.1.call-done) | data formatting | bytes 12582912
  164.9 4.4 %gather_fusion.3 = f32[256,1024]{1,0:T(8,128)S(1)} fusion(f32[1536,1024]{1,0:T(8,128)} %reshape.108, s32[1024]{0:T(1024)S(1)} %pad_clamp_fusion), kind=kCustom, calls=%fused_computation.3 | custom fusion | bytes 2098176 | tf_op jit(solution)/shard_map/gather | solution.py:92
  169.3 1.7 fusion.26
  171.0 2.9 convolution_subtract_fusion
  173.9 1.1 copy.45
  174.9 1.4 fusion.9
  176.4 11.7 %cholesky.50 = f32[128,128]{1,0:T(8,128)S(1)} custom-call(f32[128,128]{1,0:T(8,128)S(1)} %cholesky.118), custom_call_target="Cholesky" | custom-call | tf_op jit(solution)/shard_map/jit(cholesky)/cholesky | solution.py:99
  188.2 9.8 %custom-call.15 = f32[1,128,128]{1,2,0:T(8,128)S(1)} custom-call(f32[1,128,128]{2,1,0:T(8,128)S(1)} %get-tuple-element.35), custom_call_target="InvertDiagBlocksLowerTriangular" | custom-call | tf_op jit(solution)/shard_map/jit(cholesky)/cholesky | solution.py:99
  198.4 11.9 %cholesky.105 = f32[128,128]{1,0:T(8,128)S(1)} custom-call(f32[128,128]{1,0:T(8,128)S(1)} %convolution_subtract_fusion.2), custom_call_target="Cholesky" | custom-call | tf_op jit(solution)/shard_map/jit(cholesky)/cholesky | solution.py:99
  210.4 0.7 compare_reduce_fusion
  212.6 4.1 %while.1 = (s32[]{:T(128)}, f32[256,256]{1,0:T(8,128)S(1)}, s32[2,2]{1,0:T(2,128)S(1)}, f32[2,128,128]{2,1,0:T(8,128)S(1)}, s32[]{:T(128)}) while((s32[]{:T(128)}, f32[256,256]{1,0:T(8,128)S(1)}, s32[2,2]{1,0:T(2,128)S(1)}, f32[2,128,128]{2,1,0:T(8,128)S(1)}, s32[]{:T(128)}) %tuple.33), condition=%wide.while_cond, body=%wide.while_body.sunk | while | flops 2 | bytes 131189 | solution.py:100
  212.6 0.6 fusion.41
  213.2 1.4 bitcast_dynamic-update-slice_fusion.2
  214.6 0.6 fusion.41
  215.2 1.4 bitcast_dynamic-update-slice_fusion.2
  216.7 19.7 %custom-call.16 = f32[2,128,128]{1,2,0:T(8,128)S(1)} custom-call(f32[2,128,128]{2,1,0:T(8,128)S(1)} %get-tuple-element.9), custom_call_target="InvertDiagBlocksLowerTriangular" | custom-call | tf_op jit(solution)/shard_map/jit(_solve_triangular)/triangular_solve | solution.py:100
  237.6 0.6 fusion.1
  238.2 1.9 fusion.3
  240.1 1.2 pad_maximum_fusion
  241.3 2.5 reshape_reshape_reshape.4
  243.8 1.7 copy.55
  245.5 37.5 %all_to_all.39 = f32[16,32,640]{2,1,0:T(8,128)} all-to-all(f32[16,32,640]{2,1,0:T(8,128)S(1)} %bitcast.69), channel_id=1, replica_groups=mesh['row_0'=4,'row_1'=8,'row_2'=2,'col'=8] {'row_2','col'}, dimensions={0} | all-to-all | bytes 2621440 | tf_op jit(solution)/shard_map/all_to_all | solution.py:38
  283.0 1.4 reduce_sum.69
  284.5 14.5 %all_to_all.40 = f32[32,1,640]{2,1,0:T(1,128)S(1)} all-to-all(f32[32,1,640]{2,1,0:T(1,128)S(1)} %all_to_all.27), channel_id=1, replica_groups=mesh['row_0'=4,'row_1'=8,'row_2'=2,'col'=8] {'row_0','row_1'}, dimensions={0} | all-to-all | bytes 163840 | tf_op jit(solution)/shard_map/all_to_all | solution.py:45
  299.1 12.3 %all_to_all.41 = f32[32,1,640]{2,1,0:T(1,128)S(1)} all-to-all(f32[32,1,640]{2,1,0:T(1,128)S(1)} %broadcast_in_dim.79), channel_id=1, replica_groups=mesh['row_0'=4,'row_1'=8,'row_2'=2,'col'=8] {'row_0','row_1'}, dimensions={0} | all-to-all | bytes 163840 | tf_op jit(solution)/shard_map/all_to_all | solution.py:16
  311.4 1.2 broadcast_in_dim.80
  312.6 7.8 %all-to-all-start.5 = ((f32[16,32,640]{2,1,0:T(8,128)}), f32[16,32,640]{2,1,0:T(8,128)}, u32[]{:S(2)}, u32[]{:S(2)}) async-start(f32[16,32,640]{2,1,0:T(8,128)} %broadcast_in_dim.80), calls=%async_computation.5 | async-start | bytes 2621440 | tf_op jit(solution)/shard_map/all_to_all | solution.py:16
  320.4 1.0 copy.49
  321.4 31.0 %all-to-all-done.5 = f32[16,32,640]{2,1,0:T(8,128)} async-done(((f32[16,32,640]{2,1,0:T(8,128)}), f32[16,32,640]{2,1,0:T(8,128)}, u32[]{:S(2)}, u32[]{:S(2)}) %all-to-all-start.5) | async-done | bytes 1310752 | tf_op jit(solution)/shard_map/all_to_all | solution.py:16
  352.4 1.4 multiply_bitcast_fusion
  353.8 0.8 copy.48
  354.6 1.4 div.20
  (45 shorter events, 3.1 us)
Async XLA Ops:
  7.2 2.7 copy-start
  7.2 147.0 %all-gather.3.cloned.1.call-start = ((), (), s32[]{:S(2)}) async-start(), calls=%async_computation.6 | async-start | bytes 8404992 | tf_op jit(solution)/shard_map/all_gather | solution.py:89
  37.1 9.3 %copy-start.4 = (s32[256]{0:T(256)S(1)}, s32[256]{0:T(256)}, u32[]{:S(2)}) copy-start(s32[256]{0:T(256)} %param.8) | copy-start | bytes 3076
  37.1 9.4 %copy-start.1 = (bf16[512,512]{1,0:T(8,128)(2,1)S(1)}, bf16[512,512]{1,0:T(8,128)(2,1)}, u32[]{:S(2)}) copy-start(bf16[512,512]{1,0:T(8,128)(2,1)} %param.5) | copy-start | bytes 1572868
  37.1 47.4 %all-to-all-start.1 = ((bf16[16,32,3,512]{3,1,2,0:T(8,128)(2,1)}), bf16[16,32,3,512]{3,1,2,0:T(8,128)(2,1)}, u32[]{:S(2)}, u32[]{:S(2)}) async-start(bf16[16,32,3,512]{3,1,2,0:T(8,128)(2,1)} %broadcast_in_dim.75), calls=%async_computation.1 | async-start | bytes 3145728 | tf_op jit(solution)/shard_map/all_to_all | solution.py:16
  169.3 1.7 copy-start.3
  176.4 60.0 %copy-start.2 = (f32[256,512]{1,0:T(8,128)S(1)}, f32[256,512]{1,0:T(8,128)}, u32[]{:S(2)}) copy-start(f32[256,512]{1,0:T(8,128)} %convolution_subtract_fusion) | copy-start | bytes 1572868
  212.5 25.1 %copy-start.5 = (f32[512]{0:T(512)S(1)}, f32[512]{0:T(512)}, u32[]{:S(2)}) copy-start(f32[512]{0:T(512)} %param.7) | copy-start | bytes 6148
  312.6 39.8 %all-to-all-start.5 = ((f32[16,32,640]{2,1,0:T(8,128)}), f32[16,32,640]{2,1,0:T(8,128)}, u32[]{:S(2)}, u32[]{:S(2)}) async-start(f32[16,32,640]{2,1,0:T(8,128)} %broadcast_in_dim.80), calls=%async_computation.5 | async-start | bytes 2621440 | tf_op jit(solution)/shard_map/all_to_all | solution.py:16
Sparse Core Ops, SparseCore 0:
  13.0 141.0 all-gather.2
where the time goes:
time: 364 us; the launch traced here: 363 us
  waiting for transfers between devices  124 us (34%)
  blocking collectives  86.9 us (24%)
  other arithmetic  63.1 us (17%)
  local copies, waits for them, and re-layouts  45.7 us (13%)
  starting transfers between devices  17.2 us (5%)
  between operations  15.7 us (4%)
  matrix products  10.2 us (3%)
    all_to_all x2, waiting for transfers between devices, copy_for_each(): return lax.all_to_all(copies, axis, split_axis=0, concat_axis=0, tiled=True)  68.9 us
    all_gather x1, waiting for transfers between devices, body(): every_h = lax.all_gather(slot_h, ROW_COL, axis=0, tiled=True)  55.2 us
    all_to_all x1, blocking collectives, summed_on_arrival(): lax.all_to_all(parts, axis, split_axis=0, concat_axis=0, tiled=True)  37.5 us
    all_to_all x2, blocking collectives, copy_for_each(): return lax.all_to_all(copies, axis, split_axis=0, concat_axis=0, tiled=True)  34.9 us
    another operation x6, other arithmetic, body(): lower_block = jnp.linalg.cholesky(block)  34.2 us
    another operation x3, other arithmetic, body(): jax.scipy.linalg.solve_triangular(lower_block, residual.T, lower=True)  19.7 us
    all_to_all x2, starting transfers between devices, copy_for_each(): return lax.all_to_all(copies, axis, split_axis=0, concat_axis=0, tiled=True)  17.1 us
    all_to_all x1, blocking collectives, sum_by_axis(): return jnp.sum(lax.all_to_all(own, far, 0, 0, tiled=True), axis=0)  14.5 us
  transfers between devices with their start and end apart: 3, of which 3 were waited for; matrix products, arithmetic and copies ran while one was open for 5% of the time, Pallas kernels for 0%

commit v1 on v0

--- a/solution.py
+++ b/solution.py
@@ -86,7 +86,9 @@
     slot_x = jnp.where(filled, features[slot_rows], jnp.zeros((), jnp.bfloat16))
     slot_h = jnp.where(filled, factor[slot_rows], 0.0)
     every_x = gather_axes(slot_x, (("row_0", "row_1"), ("row_2", "col")), 0)
-    every_h = lax.all_gather(slot_h, ROW_COL, axis=0, tiled=True)
+    every_h = jnp.concatenate(
+        lax.all_to_all(jnp.stack([slot_h] * lax.axis_size(ROW_COL)), ROW_COL, 0, 0), axis=0
+    )
     source = pivot_owner * slot_count + slot_rank
     pivot_x = every_x[source]
     pivot_h = every_h[source]

time: 364 us -> 483 us (1.33)
  waiting for transfers between devices: 124 us -> 240 us
  between operations: 15.7 us -> 2.28 us
  starting transfers between devices: 17.2 us -> 28.3 us
  local copies, waits for them, and re-layouts: 45.7 us -> 50.9 us
    all_to_all x0 -> x1, waiting for transfers between devices: none -> 171 us  [body(): lax.all_to_all(jnp.stack([slot_h] * lax.axis_size(ROW_COL)), ROW_COL, 0, 0)]
    all_gather x1 -> x0, waiting for transfers between devices: 55.2 us -> none  [body(): every_h = lax.all_gather(slot_h, ROW_COL, axis=0, tiled=True)]
    all_to_all x0 -> x1, starting transfers between devices: none -> 11.3 us  [body(): lax.all_to_all(jnp.stack([slot_h] * lax.axis_size(ROW_COL)), ROW_COL, 0, 0)]
    reshape x0 -> x1, local copies, waits for them, and re-layouts: none -> 10.8 us  [body(): jnp.concatenate(lax.all_to_all(jnp.stack([slot_h] * lax.axis_size(ROW_COL...]
    unnamed x15 -> x14, local copies, waits for them, and re-layouts: 11.8 us -> 1.04 us
    another operation x6 -> x7, local copies, waits for them, and re-layouts: 4.06 us -> 9.41 us  [the longest x1 5.35 us: body(): jnp.stack([slot_h] * lax.axis_size(ROW_COL))]
  transfers between devices with their start and end apart: 3 -> 3, of which waited for: 3 -> 3; matrix products, arithmetic and copies ran while one was open for 5% -> 3% of each run, Pallas kernels for 0% -> 0%
where the time goes in v1:
time: 483 us; the launch traced here: 481 us
  waiting for transfers between devices  240 us (50%)
  blocking collectives  87.4 us (18%)
  other arithmetic  62.5 us (13%)
  local copies, waits for them, and re-layouts  50.9 us (11%)
  starting transfers between devices  28.3 us (6%)
  matrix products  10.2 us (2%)
    all_to_all x1, waiting for transfers between devices, body(): lax.all_to_all(jnp.stack([slot_h] * lax.axis_size(ROW_COL)), ROW_COL, 0, 0)  171 us
    all_to_all x2, waiting for transfers between devices, copy_for_each(): return lax.all_to_all(copies, axis, split_axis=0, concat_axis=0, tiled=True)  68.4 us
    all_to_all x1, blocking collectives, summed_on_arrival(): lax.all_to_all(parts, axis, split_axis=0, concat_axis=0, tiled=True)  38.3 us
    all_to_all x2, blocking collectives, copy_for_each(): return lax.all_to_all(copies, axis, split_axis=0, concat_axis=0, tiled=True)  34.9 us
    another operation x6, other arithmetic, body(): lower_block = jnp.linalg.cholesky(block)  34.2 us
    another operation x3, other arithmetic, body(): jax.scipy.linalg.solve_triangular(lower_block, residual.T, lower=True)  19.7 us
    all_to_all x2, starting transfers between devices, copy_for_each(): return lax.all_to_all(copies, axis, split_axis=0, concat_axis=0, tiled=True)  17 us
    all_to_all x1, blocking collectives, sum_by_axis(): return jnp.sum(lax.all_to_all(own, far, 0, 0, tiled=True), axis=0)  14.1 us
  transfers between devices with their start and end apart: 3, of which 3 were waited for; matrix products, arithmetic and copies ran while one was open for 3% of the time, Pallas kernels for 0%

profile of v1, /device:TPU:1, one launch (start us, length us, event | category | flops | bytes accessed | tf_op | source)
XLA Modules:
  0.0 481.3 jit_solution(16684951249152839889)
XLA Ops:
  0.6 1.0 convert_reduce_fusion
  1.7 0.7 broadcast_compare_fusion
  2.5 0.8 select_reduce_fusion.2
  3.3 1.7 gather_fusion
  5.1 22.7 %all_to_all.43 = bf16[32,3,512]{2,1,0:T(4,128)(2,1)S(1)} all-to-all(bf16[32,3,512]{2,1,0:T(4,128)(2,1)S(1)} %broadcast_in_dim.74), channel_id=1, replica_groups=mesh['row_0'=4,'row_1'=8,'row_2'=2,'col'=8] {'row_0','row_1'}, dimensions={0} | all-to-all | bytes 196608 | tf_op jit(solution)/shard_map/all_to_all | solution.py:16
  27.8 1.3 broadcast_in_dim.75
  29.1 9.2 %all-to-all-start.1 = ((bf16[16,32,3,512]{3,1,2,0:T(8,128)(2,1)}), bf16[16,32,3,512]{3,1,2,0:T(8,128)(2,1)}, u32[]{:S(2)}, u32[]{:S(2)}) async-start(bf16[16,32,3,512]{3,1,2,0:T(8,128)(2,1)} %broadcast_in_dim.75), calls=%async_computation.1 | async-start | bytes 3145728 | tf_op jit(solution)/shard_map/all_to_all | solution.py:16
  39.0 37.4 %all-to-all-done.1 = bf16[16,32,3,512]{3,1,2,0:T(8,128)(2,1)} async-done(((bf16[16,32,3,512]{3,1,2,0:T(8,128)(2,1)}), bf16[16,32,3,512]{3,1,2,0:T(8,128)(2,1)}, u32[]{:S(2)}, u32[]{:S(2)}) %all-to-all-start.1) | async-done | bytes 1572896 | tf_op jit(solution)/shard_map/all_to_all | solution.py:16
  76.4 5.3 %stack.2 = f32[512,3,1024]{2,1,0:T(4,128)} broadcast(f32[3,1024]{1,0:T(4,128)S(1)} %broadcast_select_fusion), dimensions={1,2} | broadcast | bytes 6303744 | tf_op jit(solution)/shard_map/stack | solution.py:90
  81.8 11.3 %all-to-all-start.2 = ((f32[512,3,1024]{2,1,0:T(4,128)}), f32[512,3,1024]{2,1,0:T(4,128)}, u32[]{:S(2)}, u32[]{:S(2)}) async-start(f32[512,3,1024]{2,1,0:T(4,128)} %stack.2), calls=%async_computation.2 | async-start | bytes 16777216 | tf_op jit(solution)/shard_map/all_to_all | solution.py:90
  93.3 4.1 copy.42
  97.4 5.0 %reshape_reshape.3 = bf16[1536,512]{1,0:T(8,128)(2,1)} reshape(bf16[32,16,3,512]{3,2,1,0:T(4,128)(2,1)} %copy.42) | data formatting | bytes 3145728 | tf_op jit(solution)/shard_map/reshape;reshape | solution.py:22
  102.5 2.8 gather_fusion.1
  105.6 0.8 copy.44
  106.5 1.1 fusion
  107.7 171.3 %all-to-all-done.2 = f32[512,3,1024]{2,1,0:T(4,128)} async-done(((f32[512,3,1024]{2,1,0:T(4,128)}), f32[512,3,1024]{2,1,0:T(4,128)}, u32[]{:S(2)}, u32[]{:S(2)}) %all-to-all-start.2) | async-done | bytes 6291488 | tf_op jit(solution)/shard_map/all_to_all | solution.py:90
  279.0 10.8 %reshape.64 = f32[1536,1024]{1,0:T(8,128)} reshape(f32[512,3,1024]{2,1,0:T(4,128)} %all-to-all-done.2) | data formatting | bytes 12582912 | tf_op jit(solution)/shard_map/reshape | solution.py:89
  289.7 4.4 gather_fusion.3
  294.1 1.7 fusion.26
  295.8 2.9 convolution_subtract_fusion
  298.7 1.1 copy.45
  299.8 1.4 fusion.9
  301.2 11.7 %cholesky.50 = f32[128,128]{1,0:T(8,128)S(1)} custom-call(f32[128,128]{1,0:T(8,128)S(1)} %cholesky.118), custom_call_target="Cholesky" | custom-call | tf_op jit(solution)/shard_map/jit(cholesky)/cholesky | solution.py:101
  313.0 9.8 %custom-call.15 = f32[1,128,128]{1,2,0:T(8,128)S(1)} custom-call(f32[1,128,128]{2,1,0:T(8,128)S(1)} %get-tuple-element.35), custom_call_target="InvertDiagBlocksLowerTriangular" | custom-call | tf_op jit(solution)/shard_map/jit(cholesky)/cholesky | solution.py:101
  323.3 11.9 %cholesky.105 = f32[128,128]{1,0:T(8,128)S(1)} custom-call(f32[128,128]{1,0:T(8,128)S(1)} %convolution_subtract_fusion.2), custom_call_target="Cholesky" | custom-call | tf_op jit(solution)/shard_map/jit(cholesky)/cholesky | solution.py:101
  335.2 0.7 compare_reduce_fusion
  337.4 4.1 while.1
  337.4 0.6 fusion.41
  338.0 1.4 bitcast_dynamic-update-slice_fusion.2
  339.5 0.6 fusion.41
  340.1 1.4 bitcast_dynamic-update-slice_fusion.2
  341.5 19.7 %custom-call.16 = f32[2,128,128]{1,2,0:T(8,128)S(1)} custom-call(f32[2,128,128]{2,1,0:T(8,128)S(1)} %get-tuple-element.9), custom_call_target="InvertDiagBlocksLowerTriangular" | custom-call | tf_op jit(solution)/shard_map/jit(_solve_triangular)/triangular_solve | solution.py:102
  362.4 0.6 fusion.1
  363.1 1.9 fusion.3
  365.0 1.2 pad_maximum_fusion
  366.1 2.5 reshape_reshape_reshape.4
  368.6 1.7 copy.55
  370.4 38.3 %all_to_all.44 = f32[16,32,640]{2,1,0:T(8,128)} all-to-all(f32[16,32,640]{2,1,0:T(8,128)S(1)} %bitcast.67), channel_id=1, replica_groups=mesh['row_0'=4,'row_1'=8,'row_2'=2,'col'=8] {'row_2','col'}, dimensions={0} | all-to-all | bytes 2621440 | tf_op jit(solution)/shard_map/all_to_all | solution.py:38
  408.7 1.4 reduce_sum.69
  410.2 14.1 %all_to_all.45 = f32[32,1,640]{2,1,0:T(1,128)S(1)} all-to-all(f32[32,1,640]{2,1,0:T(1,128)S(1)} %all_to_all.31), channel_id=1, replica_groups=mesh['row_0'=4,'row_1'=8,'row_2'=2,'col'=8] {'row_0','row_1'}, dimensions={0} | all-to-all | bytes 163840 | tf_op jit(solution)/shard_map/all_to_all | solution.py:45
  424.4 12.3 %all_to_all.46 = f32[32,1,640]{2,1,0:T(1,128)S(1)} all-to-all(f32[32,1,640]{2,1,0:T(1,128)S(1)} %broadcast_in_dim.79), channel_id=1, replica_groups=mesh['row_0'=4,'row_1'=8,'row_2'=2,'col'=8] {'row_0','row_1'}, dimensions={0} | all-to-all | bytes 163840 | tf_op jit(solution)/shard_map/all_to_all | solution.py:16
  436.7 1.2 broadcast_in_dim.80
  437.8 7.8 %all-to-all-start.6 = ((f32[16,32,640]{2,1,0:T(8,128)}), f32[16,32,640]{2,1,0:T(8,128)}, u32[]{:S(2)}, u32[]{:S(2)}) async-start(f32[16,32,640]{2,1,0:T(8,128)} %broadcast_in_dim.80), calls=%async_computation.6 | async-start | bytes 2621440 | tf_op jit(solution)/shard_map/all_to_all | solution.py:16
  445.7 1.0 copy.49
  446.7 31.0 %all-to-all-done.6 = f32[16,32,640]{2,1,0:T(8,128)} async-done(((f32[16,32,640]{2,1,0:T(8,128)}), f32[16,32,640]{2,1,0:T(8,128)}, u32[]{:S(2)}, u32[]{:S(2)}) %all-to-all-start.6) | async-done | bytes 1310752 | tf_op jit(solution)/shard_map/all_to_all | solution.py:16
  477.7 1.4 multiply_bitcast_fusion
  479.1 0.8 copy.48
  479.9 1.4 div.20
  (45 shorter events, 3.6 us)
Async XLA Ops:
  0.6 37.7 %copy-start = (f32[512,1024]{1,0:T(8,128)S(1)}, f32[512,1024]{1,0:T(8,128)}, u32[]{:S(2)}) copy-start(f32[512,1024]{1,0:T(8,128)} %param.6) | copy-start | bytes 6291460
  29.1 47.3 %all-to-all-start.1 = ((bf16[16,32,3,512]{3,1,2,0:T(8,128)(2,1)}), bf16[16,32,3,512]{3,1,2,0:T(8,128)(2,1)}, u32[]{:S(2)}, u32[]{:S(2)}) async-start(bf16[16,32,3,512]{3,1,2,0:T(8,128)(2,1)} %broadcast_in_dim.75), calls=%async_computation.1 | async-start | bytes 3145728 | tf_op jit(solution)/shard_map/all_to_all | solution.py:16
  81.8 11.3 %copy-start.4 = (s32[256]{0:T(256)S(1)}, s32[256]{0:T(256)}, u32[]{:S(2)}) copy-start(s32[256]{0:T(256)} %param.8) | copy-start | bytes 3076
  81.8 11.4 %copy-start.1 = (bf16[512,512]{1,0:T(8,128)(2,1)S(1)}, bf16[512,512]{1,0:T(8,128)(2,1)}, u32[]{:S(2)}) copy-start(bf16[512,512]{1,0:T(8,128)(2,1)} %param.5) | copy-start | bytes 1572868
  81.8 197.2 %all-to-all-start.2 = ((f32[512,3,1024]{2,1,0:T(4,128)}), f32[512,3,1024]{2,1,0:T(4,128)}, u32[]{:S(2)}, u32[]{:S(2)}) async-start(f32[512,3,1024]{2,1,0:T(4,128)} %stack.2), calls=%async_computation.2 | async-start | bytes 16777216 | tf_op jit(solution)/shard_map/all_to_all | solution.py:90
  294.1 1.7 copy-start.3
  301.2 60.0 %copy-start.2 = (f32[256,512]{1,0:T(8,128)S(1)}, f32[256,512]{1,0:T(8,128)}, u32[]{:S(2)}) copy-start(f32[256,512]{1,0:T(8,128)} %convolution_subtract_fusion) | copy-start | bytes 1572868
  337.3 25.1 %copy-start.5 = (f32[512]{0:T(512)S(1)}, f32[512]{0:T(512)}, u32[]{:S(2)}) copy-start(f32[512]{0:T(512)} %param.7) | copy-start | bytes 6148
  437.8 39.8 %all-to-all-start.6 = ((f32[16,32,640]{2,1,0:T(8,128)}), f32[16,32,640]{2,1,0:T(8,128)}, u32[]{:S(2)}, u32[]{:S(2)}) async-start(f32[16,32,640]{2,1,0:T(8,128)} %broadcast_in_dim.80), calls=%async_computation.6 | async-start | bytes 2621440 | tf_op jit(solution)/shard_map/all_to_all | solution.py:16
